TPU v7x, 32 devices: a whole 2x2x4 slice. The times are simulated.
32 devices in a mesh: group: 2 (over x), inner: 16 (over z, y, core).
Axes of the slice: x: 2, y: 2, z: 4, core: 2. Of those that a mesh axis runs over, the one named last changes fastest.
Arguments:
- qkv_rows: bfloat16 [4096, 2304], P(('group', 'inner')), parts along dimension 0, may hold values from -8 to 8
- pair_counts: int32 [32, 16], P('group'), parts along dimension 0, may hold values from 0 to 16, as said below
- image_dims: int32 [2, 32], P(None, 'group'), parts along dimension 1, may hold values from 0 to 4, as said below
- block_mask: int32 [32, 7], P(('group', 'inner')), parts along dimension 0, may hold values from 0 to 1, as said below
- out_weight: bfloat16 [768, 1536], replicated, may hold values from -0.21875 to 0.21875
Outputs:
- layer_out: bfloat16 [4096, 1536], P(('group', 'inner')), parts along dimension 0
There are 2 independent parts, one for each index of `group`. A program takes and returns all parts, laid end to end along the dimension named above; an argument that names none is the same for every part. Nothing has to cross between parts.
Inputs may be any that keep to these rules, and one draw needn't show every extreme that they name: `pair_counts`: every row and every column sums to 128, and every row and every column holds an entry equal to 16. `image_dims`: widths are 1, 2 or 4; each image covers at most 4 tiles and some image is 4 tiles high and 1 wide; the tiles of all images sum to 16; images of height 0 stand only after all others. `block_mask`: column 4 - 1 (a tile with itself) is always 1.
All inputs are finite; a program needn't handle non-finite values.
Results may differ from a plain program's by a relative error of at most 0.0093.
Values may be sent and summed in bfloat16 or wider, within the bound.
A program may use at most 64 MiB of HBM per device.

v0:
```python
import math

import jax
import jax.numpy as jnp
from jax import lax
from jax.sharding import PartitionSpec as P

H = 6
HD = 128
TR = 8
TC = 16
SPAN = 4
MAXT = 4
WIN = 7


def from_behind(value, axis, steps):
    count = lax.axis_size(axis)
    pairs = [(source, (source + steps) % count) for source in range(count)]
    return lax.ppermute(value, axis, pairs)


def block_places(blocks, image_dims):
    heights = image_dims[0]
    widths = image_dims[1]
    tile_count = heights * widths
    starts = jnp.cumsum(tile_count) - tile_count
    inside = (starts[None, :] <= blocks[:, None]).astype(jnp.int32)
    image_id = jnp.sum(inside, axis=1) - 1
    picked = jnp.arange(starts.shape[0], dtype=jnp.int32)[None, :] == image_id[:, None]
    first_block = jnp.sum(jnp.where(picked, starts[None, :], 0), axis=1)
    across = jnp.maximum(jnp.sum(jnp.where(picked, widths[None, :], 0), axis=1), 1)
    local_tile = blocks - first_block
    return (image_id, local_tile // across, local_tile % across)


def rotate(rows_in, row_pos, col_pos):
    count = rows_in.shape[0]
    quarter = HD // 4
    frequency = 10000.0 ** (-jnp.arange(quarter, dtype=jnp.float32) / quarter)
    angles = jnp.stack(
        [
            row_pos.astype(jnp.float32)[:, None] * frequency[None, :],
            col_pos.astype(jnp.float32)[:, None] * frequency[None, :],
        ],
        axis=1,
    )
    cosine = jnp.cos(angles)[:, None, :, :]
    sine_part = jnp.sin(angles)[:, None, :, :]
    split_rows = rows_in.astype(jnp.float32).reshape(count, H, 2, 2, quarter)
    leading = split_rows[:, :, :, 0, :]
    trailing = split_rows[:, :, :, 1, :]
    turned = jnp.stack(
        [leading * cosine - trailing * sine_part, trailing * cosine + leading * sine_part], axis=3
    )
    return turned.reshape(count, H * HD).astype(jnp.bfloat16)


def shards(qkv_rows, pair_counts, image_dims, block_mask, out_weight):
    devices = lax.axis_size("inner")
    self_index = lax.axis_index("inner")
    tok_rows = qkv_rows.shape[0]
    full_width = qkv_rows.shape[1]
    inner_width = full_width // 3
    slot_count = 2 * tok_rows // devices
    block_rows = TR * TC
    per_device = tok_rows // block_rows
    reach_count = (SPAN * tok_rows - block_rows + tok_rows - 1) // tok_rows
    score_scale = 1.0 / math.sqrt(HD)
    sent_counts = lax.dynamic_index_in_dim(pair_counts, self_index, 0, keepdims=False)
    taken_counts = lax.dynamic_index_in_dim(pair_counts, self_index, 1, keepdims=False)
    sent_end = jnp.cumsum(sent_counts)
    sent_start = sent_end - sent_counts
    taken_end = jnp.cumsum(taken_counts)
    taken_start = taken_end - taken_counts
    slot_ids = jnp.arange(slot_count, dtype=jnp.int32)
    row_ids = jnp.arange(tok_rows, dtype=jnp.int32)
    peer_ids = jnp.arange(devices, dtype=jnp.int32)
    outgoing = jnp.minimum(sent_start[:, None] + slot_ids[None, :], tok_rows - 1).reshape(-1)
    parcels = jnp.take(qkv_rows, outgoing, axis=0).reshape(devices, slot_count, full_width)
    arrived = lax.all_to_all(parcels, "inner", split_axis=0, concat_axis=0, tiled=True)
    source = jnp.sum((taken_end[None, :] <= row_ids[:, None]).astype(jnp.int32), axis=1)
    is_source = source[:, None] == peer_ids[None, :]
    offset_in = row_ids - jnp.sum(jnp.where(is_source, taken_start[None, :], 0), axis=1)
    incoming = source * slot_count + offset_in
    owned_rows = jnp.take(arrived.reshape(devices * slot_count, full_width), incoming, axis=0)
    query_blocks = self_index * per_device + jnp.arange(per_device, dtype=jnp.int32)
    query_image, tile_row, tile_col = block_places(query_blocks, image_dims)
    within = jnp.arange(block_rows, dtype=jnp.int32)
    row_pos = (tile_row[:, None] * TR + within[None, :] // TC).reshape(-1)
    col_pos = (tile_col[:, None] * TC + within[None, :] % TC).reshape(-1)
    queries = rotate(owned_rows[:, :inner_width], row_pos, col_pos).reshape(tok_rows, H, HD)
    keys = rotate(owned_rows[:, inner_width : 2 * inner_width], row_pos, col_pos)
    key_value = jnp.stack([keys, owned_rows[:, 2 * inner_width :]])

    def absorb(softmax_state, key_piece, allowed):
        row_max, row_sum, summed = softmax_state
        visible = jnp.repeat(jnp.repeat(allowed, block_rows, axis=0), block_rows, axis=1)[
            :, None, :
        ]
        far_keys = key_piece[0].reshape(tok_rows, H, HD)
        far_values = key_piece[1].reshape(tok_rows, H, HD)
        scores = (
            jnp.einsum("qhd,khd->qhk", queries, far_keys, preferred_element_type=jnp.float32)
            * score_scale
        )
        scores = jnp.where(visible, scores, -1e30)
        new_max = jnp.maximum(row_max, jnp.max(scores, axis=2))
        weights = jnp.where(visible, jnp.exp(scores - new_max[:, :, None]), 0.0)
        rescale = jnp.exp(row_max - new_max)
        row_sum = row_sum * rescale + jnp.sum(weights, axis=2)
        summed = summed * rescale[:, :, None] + jnp.einsum(
            "qhk,khd->qhd",
            weights.astype(jnp.bfloat16),
            far_values,
            preferred_element_type=jnp.float32,
        )
        return (new_max, row_sum, summed)

    def visit(softmax_state, key_piece, source_dev):
        key_blocks = source_dev * per_device + jnp.arange(per_device, dtype=jnp.int32)
        key_image = block_places(key_blocks, image_dims)[0]
        offset = key_blocks[None, :] - query_blocks[:, None] + (MAXT - 1)
        mask_bits = jnp.take_along_axis(block_mask, jnp.clip(offset, 0, WIN - 1), axis=1)
        allowed = (
            (offset >= 0)
            & (offset < WIN)
            & (mask_bits == 1)
            & (query_image[:, None] == key_image[None, :])
            & (source_dev >= 0)
            & (source_dev < devices)
        )
        return absorb(softmax_state, key_piece, allowed)

    initial = (
        jnp.full((tok_rows, H), -1e30, jnp.float32),
        jnp.zeros((tok_rows, H), jnp.float32),
        jnp.zeros((tok_rows, H, HD), jnp.float32),
    )
    farthest = from_behind(key_value, "inner", -reach_count)
    softmax_state = visit(initial, farthest, self_index + reach_count)

    def one_way(hop_index, carry):
        key_piece, running = carry
        key_piece = from_behind(key_piece, "inner", 1)
        return (key_piece, visit(running, key_piece, self_index + reach_count - hop_index - 1))

    softmax_state = lax.fori_loop(0, 2 * reach_count, one_way, (farthest, softmax_state))[1]
    row_max, row_sum, summed = softmax_state
    attended = (summed / row_sum[:, :, None]).reshape(tok_rows, H * HD).astype(jnp.bfloat16)
    projected = jnp.dot(attended, out_weight, preferred_element_type=jnp.float32).astype(
        jnp.bfloat16
    )
    out_width = projected.shape[1]
    back_slots = jnp.minimum(taken_start[:, None] + slot_ids[None, :], tok_rows - 1).reshape(-1)
    returning = jnp.take(projected, back_slots, axis=0).reshape(devices, slot_count, out_width)
    returned = lax.all_to_all(returning, "inner", split_axis=0, concat_axis=0, tiled=True)
    target = jnp.sum((sent_end[None, :] <= row_ids[:, None]).astype(jnp.int32), axis=1)
    is_target = target[:, None] == peer_ids[None, :]
    offset_back = row_ids - jnp.sum(jnp.where(is_target, sent_start[None, :], 0), axis=1)
    return jnp.take(
        returned.reshape(devices * slot_count, out_width), target * slot_count + offset_back, axis=0
    )


def solution(mesh):
    in_specs = (
        P(("group", "inner"), None),
        P("group", None),
        P(None, "group"),
        P(("group", "inner"), None),
        P(),
    )
    out_specs = P(("group", "inner"), None)
    return jax.shard_map(shards, mesh=mesh, in_specs=in_specs, out_specs=out_specs, check_vma=False)
```

profile of v0, /device:TPU:0, one launch (start us, length us, event | category | flops | bytes accessed | tf_op | source)
XLA Modules:
  0.0 164.5 jit_solution(5951095822573143242)
XLA Ops:
  2.5 3.7 %gather_fusion = bf16[256,2304]{1,0:T(8,128)(2,1)S(1)} fusion(bf16[128,2304]{1,0:T(8,128)(2,1)} %param.7, s32[1024]{0:T(1024)S(1)} %pad_clamp_fusion.3), kind=kCustom, calls=%fused_computation | custom fusion | bytes 2360320 | tf_op jit(solution)/shard_map/jit(_take)/gather | solution.py:80
  6.3 1.2 broadcast_select_fusion
  7.4 7.5 %all-to-all-start = ((bf16[16,16,2304]{2,1,0:T(8,128)(2,1)}), bf16[16,16,2304]{2,1,0:T(8,128)(2,1)S(1)}, u32[]{:S(2)}, u32[]{:S(2)}) async-start(bf16[16,16,2304]{2,1,0:T(8,128)(2,1)} %broadcast_select_fusion), calls=%async_computation | async-start | bytes 2359296 | tf_op jit(solution)/shard_map/all_to_all | solution.py:81
  15.7 1.4 fusion.28
  27.4 12.7 %all-to-all-done = bf16[16,16,2304]{2,1,0:T(8,128)(2,1)S(1)} async-done(((bf16[16,16,2304]{2,1,0:T(8,128)(2,1)}), bf16[16,16,2304]{2,1,0:T(8,128)(2,1)S(1)}, u32[]{:S(2)}, u32[]{:S(2)}) %all-to-all-start) | async-done | bytes 1179680 | tf_op jit(solution)/shard_map/all_to_all | solution.py:81
  40.1 1.8 %gather_fusion.1 = bf16[128,2304]{1,0:T(8,128)(2,1)} fusion(bf16[256,2304]{1,0:T(8,128)(2,1)S(1)} %bitcast.110, s32[1024]{0:T(1024)S(1)} %pad_clamp_fusion.2), kind=kCustom, calls=%fused_computation.1 | custom fusion | bytes 1180160 | tf_op jit(solution)/shard_map/jit(_take)/gather | solution.py:86
  41.9 1.2 broadcast_select_fusion.2
  44.2 1.6 subtract_convert_fusion
  46.7 4.0 %collective-permute-start.1 = (bf16[2,128,768]{2,1,0:T(8,128)(2,1)}, bf16[2,128,768]{2,1,0:T(8,128)(2,1)S(1)}, u32[]{:S(2)}, u32[]{:S(2)}) collective-permute-start(bf16[2,128,768]{2,1,0:T(8,128)(2,1)} %pad_maximum_fusion), channel_id=1, source_target_pairs={{0,13},{1,14},{2,15},{3,0},{4,1},{5,2},{6,3},{7,4},{8,5},{9,6},{10... | collective-permute-start | bytes 1179656 | tf_op jit(solution)/shard_map/ppermute | solution.py:20
  54.1 4.8 %collective-permute-done.1 = bf16[2,128,768]{2,1,0:T(8,128)(2,1)S(1)} collective-permute-done((bf16[2,128,768]{2,1,0:T(8,128)(2,1)}, bf16[2,128,768]{2,1,0:T(8,128)(2,1)S(1)}, u32[]{:S(2)}, u32[]{:S(2)}) %collective-permute-start.1) | collective-permute-done | bytes 393248 | tf_op jit(solution)/shard_map/ppermute | solution.py:20
  60.5 1.2 fusion.42
  63.5 1.6 %fusion.11 = f32[128,6,128]{0,2,1:T(8,128)} fusion(bf16[128,6,128]{0,2,1:T(8,128)(2,1)S(1)} %bitcast.120, f32[128,6,128]{0,2,1:T(8,128)S(1)} %get-tuple-element.379, f32[128,6]{0,1:T(8,128)} %get-tuple-element.374, f32[128,6]{0,1:T(8,128)S(1)} %broadcast_maximum_fusion, pred[]{:T(512)} %bitcast.32), kind=kOutput, calls=%fused_computation.23 | convolution fusion | flops 25559040 | bytes 989185 | tf_op jit(solution)/shard_map/qhk,khd->qhd/dot_general | solution.py:112
  65.1 1.2 copy.45
  67.2 69.9 %while.24 = (s32[]{:T(128)}, bf16[2,128,768]{1,2,0:T(8,128)(2,1)}, f32[128,6]{0,1:T(8,128)S(1)}, f32[128,6]{0,1:T(8,128)S(1)}, f32[128,6,128]{2,0,1:T(8,128)S(1)...) while((s32[]{:T(128)}, bf16[2,128,768]{1,2,0:T(8,128)(2,1)}, ...), condition=%wide.region_17.18_spmd, body=%wide.region_13.17_spmd.sunk | while | flops 51414596 | bytes 5751247 | solution.py:148
  67.2 1.7 %collective-permute-start = (bf16[2,128,768]{1,2,0:T(8,128)(2,1)}, bf16[2,128,768]{1,2,0:T(8,128)(2,1)S(1)}, u32[]{:S(2)}, u32[]{:S(2)}) collective-permute-start(bf16[2,128,768]{1,2,0:T(8,128)(2,1)} %get-tuple-element.481), channel_id=1, source_target_pairs={{0,1},{1,2},{2,3},{3,4},{4,5},{5,6},{6,7},{7,8},{8,9},{9,10},{10,1... | collective-permute-start | bytes 1179656 | tf_op jit(solution)/shard_map/while/body/eval_jaxpr/ppermute | solution.py:20
  71.5 5.9 %collective-permute-done = bf16[2,128,768]{1,2,0:T(8,128)(2,1)S(1)} collective-permute-done((bf16[2,128,768]{1,2,0:T(8,128)(2,1)}, bf16[2,128,768]{1,2,0:T(8,128)(2,1)S(1)}, u32[]{:S(2)}, u32[]{:S(2)}) %collective-permute-start) | collective-permute-done | bytes 393248 | tf_op jit(solution)/shard_map/while/body/eval_jaxpr/ppermute | solution.py:20
  81.4 7.6 %collective-permute-done = bf16[2,128,768]{1,2,0:T(8,128)(2,1)S(1)} collective-permute-done((bf16[2,128,768]{1,2,0:T(8,128)(2,1)}, bf16[2,128,768]{1,2,0:T(8,128)(2,1)S(1)}, u32[]{:S(2)}, u32[]{:S(2)}) %collective-permute-start) | collective-permute-done | bytes 393248 | tf_op jit(solution)/shard_map/while/body/eval_jaxpr/ppermute | solution.py:20
  93.1 7.6 %collective-permute-done = bf16[2,128,768]{1,2,0:T(8,128)(2,1)S(1)} collective-permute-done((bf16[2,128,768]{1,2,0:T(8,128)(2,1)}, bf16[2,128,768]{1,2,0:T(8,128)(2,1)S(1)}, u32[]{:S(2)}, u32[]{:S(2)}) %collective-permute-start) | collective-permute-done | bytes 393248 | tf_op jit(solution)/shard_map/while/body/eval_jaxpr/ppermute | solution.py:20
  104.7 7.6 %collective-permute-done = bf16[2,128,768]{1,2,0:T(8,128)(2,1)S(1)} collective-permute-done((bf16[2,128,768]{1,2,0:T(8,128)(2,1)}, bf16[2,128,768]{1,2,0:T(8,128)(2,1)S(1)}, u32[]{:S(2)}, u32[]{:S(2)}) %collective-permute-start) | collective-permute-done | bytes 393248 | tf_op jit(solution)/shard_map/while/body/eval_jaxpr/ppermute | solution.py:20
  116.3 7.6 %collective-permute-done = bf16[2,128,768]{1,2,0:T(8,128)(2,1)S(1)} collective-permute-done((bf16[2,128,768]{1,2,0:T(8,128)(2,1)}, bf16[2,128,768]{1,2,0:T(8,128)(2,1)S(1)}, u32[]{:S(2)}, u32[]{:S(2)}) %collective-permute-start) | collective-permute-done | bytes 393248 | tf_op jit(solution)/shard_map/while/body/eval_jaxpr/ppermute | solution.py:20
  128.0 7.6 %collective-permute-done = bf16[2,128,768]{1,2,0:T(8,128)(2,1)S(1)} collective-permute-done((bf16[2,128,768]{1,2,0:T(8,128)(2,1)}, bf16[2,128,768]{1,2,0:T(8,128)(2,1)S(1)}, u32[]{:S(2)}, u32[]{:S(2)}) %collective-permute-start) | collective-permute-done | bytes 393248 | tf_op jit(solution)/shard_map/while/body/eval_jaxpr/ppermute | solution.py:20
  137.9 1.4 gather_fusion.2
  140.3 3.7 %all-to-all-start.1 = ((bf16[16,16,1536]{2,1,0:T(8,128)(2,1)}), bf16[16,16,1536]{2,1,0:T(8,128)(2,1)S(1)}, u32[]{:S(2)}, u32[]{:S(2)}) async-start(bf16[16,16,1536]{2,1,0:T(8,128)(2,1)} %broadcast_select_fusion.1), calls=%async_computation.1 | async-start | bytes 1572864 | tf_op jit(solution)/shard_map/all_to_all | solution.py:157
  144.3 18.4 %all-to-all-done.1 = bf16[16,16,1536]{2,1,0:T(8,128)(2,1)S(1)} async-done(((bf16[16,16,1536]{2,1,0:T(8,128)(2,1)}), bf16[16,16,1536]{2,1,0:T(8,128)(2,1)S(1)}, u32[]{:S(2)}, u32[]{:S(2)}) %all-to-all-start.1) | async-done | bytes 786464 | tf_op jit(solution)/shard_map/all_to_all | solution.py:157
  (155 shorter events, 40.0 us)
Async XLA Ops:
  0.0 137.3 %copy-start = (bf16[768,1536]{1,0:T(8,128)(2,1)S(1)}, bf16[768,1536]{1,0:T(8,128)(2,1)}, u32[]{:S(2)}) copy-start(bf16[768,1536]{1,0:T(8,128)(2,1)} %param.11) | copy-start | bytes 7077892
  1.1 0.5 copy-start.10
  7.4 7.5 %copy-start.14 = (s32[2,16]{1,0:T(2,128)S(1)}, s32[2,16]{1,0:T(2,128)}, u32[]{:S(2)}) copy-start(s32[2,16]{1,0:T(2,128)} %param.9) | copy-start | bytes 388
  7.4 12.9 %copy-start.4 = (s32[16,16]{1,0:T(8,128)S(1)}, s32[16,16]{1,0:T(8,128)}, u32[]{:S(2)}) copy-start(s32[16,16]{1,0:T(8,128)} %param.8) | copy-start | bytes 3076
  7.4 32.7 %all-to-all-start = ((bf16[16,16,2304]{2,1,0:T(8,128)(2,1)}), bf16[16,16,2304]{2,1,0:T(8,128)(2,1)S(1)}, u32[]{:S(2)}, u32[]{:S(2)}) async-start(bf16[16,16,2304]{2,1,0:T(8,128)(2,1)} %broadcast_select_fusion), calls=%async_computation | async-start | bytes 2359296 | tf_op jit(solution)/shard_map/all_to_all | solution.py:81
  17.0 3.3 %copy-start.12 = (s32[1,16]{1,0:T(1,128)}, s32[1,16]{1,0:T(1,128)S(1)}, u32[]{:S(2)}) copy-start(s32[1,16]{1,0:T(1,128)S(1)} %get-tuple-element.469) | copy-start | bytes 196
  22.5 0.5 copy-start.8
  44.1 1.8 %copy-start.1 = (bf16[1,128,768]{2,1,0:T(8,128)(2,1)S(1)}, bf16[1,128,768]{2,1,0:T(8,128)(2,1)}, u32[]{:S(2)}) copy-start(bf16[1,128,768]{2,1,0:T(8,128)(2,1)} %get-tuple-element.362) | copy-start | bytes 589828
  44.2 7.2 %copy-start.5 = (s32[1,7]{1,0:T(1,128)S(1)}, s32[1,7]{1,0:T(1,128)}, u32[]{:S(2)}) copy-start(s32[1,7]{1,0:T(1,128)} %param.10) | copy-start | bytes 88
  44.2 9.1 %copy-start.9 = (s32[16]{0:T(128)S(1)}, s32[16]{0:T(128)}, u32[]{:S(2)}) copy-start(s32[16]{0:T(128)} %copy-done.8) | copy-start | bytes 196
  45.8 8.1 %copy-start.2 = (bf16[128,6,2,1,32]{0,4,3,2,1:T(8,128)(2,1)S(1)}, bf16[128,6,2,1,32]{0,4,3,2,1:T(8,128)(2,1)}, u32[]{:S(2)}) copy-start(bf16[128,6,2,1,32]{0,4,3,2,1:T(8,128)(2,1)} %get-tuple-element.364) | copy-start | bytes 294916
  45.8 8.1 %copy-start.3 = (bf16[128,6,2,1,32]{0,4,3,2,1:T(8,128)(2,1)S(1)}, bf16[128,6,2,1,32]{0,4,3,2,1:T(8,128)(2,1)}, u32[]{:S(2)}) copy-start(bf16[128,6,2,1,32]{0,4,3,2,1:T(8,128)(2,1)} %get-tuple-element.365) | copy-start | bytes 294916
  46.7 12.2 %collective-permute-start.1 = (bf16[2,128,768]{2,1,0:T(8,128)(2,1)}, bf16[2,128,768]{2,1,0:T(8,128)(2,1)S(1)}, u32[]{:S(2)}, u32[]{:S(2)}) collective-permute-start(bf16[2,128,768]{2,1,0:T(8,128)(2,1)} %pad_maximum_fusion), channel_id=1, source_target_pairs={{0,13},{1,14},{2,15},{3,0},{4,1},{5,2},{6,3},{7,4},{8,5},{9,6},{10... | collective-permute-start | bytes 1179656 | tf_op jit(solution)/shard_map/ppermute | solution.py:20
  65.1 2.1 %copy-start.6 = (s32[1,7]{1,0:T(1,128)S(1)}, s32[1,7]{1,0:T(1,128)}, u32[]{:S(2)}) copy-start(s32[1,7]{1,0:T(1,128)} %param.10) | copy-start | bytes 88
  65.1 2.1 %copy-start.13 = (s32[1,16]{1,0:T(1,128)S(1)}, s32[1,16]{1,0:T(1,128)}, u32[]{:S(2)}) copy-start(s32[1,16]{1,0:T(1,128)} %copy-done.12) | copy-start | bytes 196
  67.2 10.1 %collective-permute-start = (bf16[2,128,768]{1,2,0:T(8,128)(2,1)}, bf16[2,128,768]{1,2,0:T(8,128)(2,1)S(1)}, u32[]{:S(2)}, u32[]{:S(2)}) collective-permute-start(bf16[2,128,768]{1,2,0:T(8,128)(2,1)} %get-tuple-element.481), channel_id=1, source_target_pairs={{0,1},{1,2},{2,3},{3,4},{4,5},{5,6},{6,7},{7,8},{8,9},{9,10},{10,1... | collective-permute-start | bytes 1179656 | tf_op jit(solution)/shard_map/while/body/eval_jaxpr/ppermute | solution.py:20
  78.9 10.1 %collective-permute-start = (bf16[2,128,768]{1,2,0:T(8,128)(2,1)}, bf16[2,128,768]{1,2,0:T(8,128)(2,1)S(1)}, u32[]{:S(2)}, u32[]{:S(2)}) collective-permute-start(bf16[2,128,768]{1,2,0:T(8,128)(2,1)} %get-tuple-element.481), channel_id=1, source_target_pairs={{0,1},{1,2},{2,3},{3,4},{4,5},{5,6},{6,7},{7,8},{8,9},{9,10},{10,1... | collective-permute-start | bytes 1179656 | tf_op jit(solution)/shard_map/while/body/eval_jaxpr/ppermute | solution.py:20
  90.5 10.1 %collective-permute-start = (bf16[2,128,768]{1,2,0:T(8,128)(2,1)}, bf16[2,128,768]{1,2,0:T(8,128)(2,1)S(1)}, u32[]{:S(2)}, u32[]{:S(2)}) collective-permute-start(bf16[2,128,768]{1,2,0:T(8,128)(2,1)} %get-tuple-element.481), channel_id=1, source_target_pairs={{0,1},{1,2},{2,3},{3,4},{4,5},{5,6},{6,7},{7,8},{8,9},{9,10},{10,1... | collective-permute-start | bytes 1179656 | tf_op jit(solution)/shard_map/while/body/eval_jaxpr/ppermute | solution.py:20
  102.2 10.1 %collective-permute-start = (bf16[2,128,768]{1,2,0:T(8,128)(2,1)}, bf16[2,128,768]{1,2,0:T(8,128)(2,1)S(1)}, u32[]{:S(2)}, u32[]{:S(2)}) collective-permute-start(bf16[2,128,768]{1,2,0:T(8,128)(2,1)} %get-tuple-element.481), channel_id=1, source_target_pairs={{0,1},{1,2},{2,3},{3,4},{4,5},{5,6},{6,7},{7,8},{8,9},{9,10},{10,1... | collective-permute-start | bytes 1179656 | tf_op jit(solution)/shard_map/while/body/eval_jaxpr/ppermute | solution.py:20
  113.8 10.1 %collective-permute-start = (bf16[2,128,768]{1,2,0:T(8,128)(2,1)}, bf16[2,128,768]{1,2,0:T(8,128)(2,1)S(1)}, u32[]{:S(2)}, u32[]{:S(2)}) collective-permute-start(bf16[2,128,768]{1,2,0:T(8,128)(2,1)} %get-tuple-element.481), channel_id=1, source_target_pairs={{0,1},{1,2},{2,3},{3,4},{4,5},{5,6},{6,7},{7,8},{8,9},{9,10},{10,1... | collective-permute-start | bytes 1179656 | tf_op jit(solution)/shard_map/while/body/eval_jaxpr/ppermute | solution.py:20
  125.5 10.1 %collective-permute-start = (bf16[2,128,768]{1,2,0:T(8,128)(2,1)}, bf16[2,128,768]{1,2,0:T(8,128)(2,1)S(1)}, u32[]{:S(2)}, u32[]{:S(2)}) collective-permute-start(bf16[2,128,768]{1,2,0:T(8,128)(2,1)} %get-tuple-element.481), channel_id=1, source_target_pairs={{0,1},{1,2},{2,3},{3,4},{4,5},{5,6},{6,7},{7,8},{8,9},{9,10},{10,1... | collective-permute-start | bytes 1179656 | tf_op jit(solution)/shard_map/while/body/eval_jaxpr/ppermute | solution.py:20
  137.8 1.4 copy-start.7
  140.3 3.8 %copy-start.11 = (s32[16]{0:T(128)S(1)}, s32[16]{0:T(128)}, u32[]{:S(2)}) copy-start(s32[16]{0:T(128)} %copy-done.10) | copy-start | bytes 196
  140.3 22.4 %all-to-all-start.1 = ((bf16[16,16,1536]{2,1,0:T(8,128)(2,1)}), bf16[16,16,1536]{2,1,0:T(8,128)(2,1)S(1)}, u32[]{:S(2)}, u32[]{:S(2)}) async-start(bf16[16,16,1536]{2,1,0:T(8,128)(2,1)} %broadcast_select_fusion.1), calls=%async_computation.1 | async-start | bytes 1572864 | tf_op jit(solution)/shard_map/all_to_all | solution.py:157
where the time goes:
time: 165 us; the launch traced here: 164 us
  waiting for transfers between devices  79.8 us (48%)
  other arithmetic  27.2 us (16%)
  local copies, waits for them, and re-layouts  21.9 us (13%)
  starting transfers between devices  17 us (10%)
  loops' own time  7.9 us (5%)
  matrix products  7.07 us (4%)
  between operations  3.55 us (2%)
    ppermute x7, waiting for transfers between devices, from_behind(): return lax.ppermute(value, axis, pairs)  48.6 us
    all_to_all x1, waiting for transfers between devices, shards(): lax.all_to_all(returning, 'inner', split_axis=0, concat_axis=0, tiled=True)  18.4 us
    all_to_all x1, waiting for transfers between devices, shards(): lax.all_to_all(parcels, 'inner', split_axis=0, concat_axis=0, tiled=True)  12.7 us
    another operation x1, loops' own time, shards(): lax.fori_loop(0, 2 * reach_count, one_way, (farthest, softmax_state))[1]  7.9 us
    all_to_all x1, starting transfers between devices, shards(): lax.all_to_all(parcels, 'inner', split_axis=0, concat_axis=0, tiled=True)  7.52 us
    reduce_sum x8, other arithmetic, block_places(): image_id = jnp.sum(inside, axis=1) - 1  5.9 us
    ppermute x7, starting transfers between devices, from_behind(): return lax.ppermute(value, axis, pairs)  5.73 us
    while x12, local copies, waits for them, and re-layouts  4.51 us
  transfers between devices with their start and end apart: 9, of which 9 were waited for; matrix products, arithmetic and copies ran while one was open for 12% of the time, Pallas kernels for 0%

commit v1 on v0

--- a/solution.py
+++ b/solution.py
@@ -1,8 +1,12 @@
+import functools
 import math
 
 import jax
 import jax.numpy as jnp
+import numpy as np
 from jax import lax
+from jax.experimental import pallas as pl
+from jax.experimental.pallas import tpu as pltpu
 from jax.sharding import PartitionSpec as P
 
 H = 6
@@ -14,6 +18,11 @@
 WIN = 7
 
 
+def running(counts):
+    ids = jnp.arange(counts.shape[0], dtype=jnp.int32)
+    return jnp.sum(jnp.where(ids[:, None] <= ids[None, :], counts[:, None], 0), axis=0)
+
+
 def from_behind(value, axis, steps):
     count = lax.axis_size(axis)
     pairs = [(source, (source + steps) % count) for source in range(count)]
@@ -24,7 +33,7 @@
     heights = image_dims[0]
     widths = image_dims[1]
     tile_count = heights * widths
-    starts = jnp.cumsum(tile_count) - tile_count
+    starts = running(tile_count) - tile_count
     inside = (starts[None, :] <= blocks[:, None]).astype(jnp.int32)
     image_id = jnp.sum(inside, axis=1) - 1
     picked = jnp.arange(starts.shape[0], dtype=jnp.int32)[None, :] == image_id[:, None]
@@ -69,9 +78,9 @@
     score_scale = 1.0 / math.sqrt(HD)
     sent_counts = lax.dynamic_index_in_dim(pair_counts, self_index, 0, keepdims=False)
     taken_counts = lax.dynamic_index_in_dim(pair_counts, self_index, 1, keepdims=False)
-    sent_end = jnp.cumsum(sent_counts)
+    sent_end = running(sent_counts)
     sent_start = sent_end - sent_counts
-    taken_end = jnp.cumsum(taken_counts)
+    taken_end = running(taken_counts)
     taken_start = taken_end - taken_counts
     slot_ids = jnp.arange(slot_count, dtype=jnp.int32)
     row_ids = jnp.arange(tok_rows, dtype=jnp.int32)
@@ -163,7 +172,354 @@
     )
 
 
+ROWS = TR * TC
+EXTRA = 16
+HIDDEN = -1e30
+MESH_ID = pl.DeviceIdType.MESH
+
+
+def nt_dot(a, b):
+    return lax.dot_general(a, b, (((1,), (1,)), ((), ())), preferred_element_type=jnp.float32)
+
+
+def nn_dot(a, b):
+    return jnp.dot(a, b, preferred_element_type=jnp.float32)
+
+
+def iota(shape, dim):
+    return lax.broadcasted_iota(jnp.int32, shape, dim)
+
+
+def head_kernel(
+    devices,
+    qkv_ref,
+    pair_ref,
+    dims_ref,
+    mask_ref,
+    freq_ref,
+    out_ref,
+    q_out,
+    k_out,
+    q_in,
+    k_in,
+    v_in,
+    tile_of,
+    starts_ref,
+    ends_ref,
+    bias_ref,
+    weights_ref,
+    sum_ref,
+    total_ref,
+    done_ref,
+    home_ref,
+    send_sem,
+    recv_sem,
+    pass_send_sem,
+    pass_recv_sem,
+    back_send_sem,
+    back_recv_sem,
+):
+    me = lax.axis_index("inner")
+    group = lax.axis_index("group")
+    chips = devices // 2
+    chip = me // 2
+    core = me % 2
+    sibling = chip * 2 + (1 - core)
+    first_chip = (chips - H) // 2
+    head = chip - first_chip
+    has_head = (head >= 0) & (head < H)
+
+    def device(index):
+        return (group, index)
+
+    barrier = pltpu.get_barrier_semaphore()
+    for hop in range(1, chips):
+        pl.semaphore_signal(
+            barrier, inc=1, device_id=device((chip ^ hop) * 2 + core), device_id_type=MESH_ID
+        )
+    pl.semaphore_signal(barrier, inc=1, device_id=device(sibling), device_id_type=MESH_ID)
+
+    src = iota((devices, 128), 0)
+    dst = iota((devices, 128), 1)
+    pairs = pair_ref[...].astype(jnp.float32).astype(jnp.bfloat16)
+    ends = nn_dot(pairs, jnp.where(src <= dst, 1.0, 0.0).astype(jnp.bfloat16))
+    starts = nn_dot(pairs, jnp.where(src < dst, 1.0, 0.0).astype(jnp.bfloat16))
+    wide = nn_dot(pairs, jnp.where(src == dst, 1.0, 0.0).astype(jnp.bfloat16))
+    below = jnp.where(iota((devices, devices), 1) < iota((devices, devices), 0), 1.0, 0.0)
+    column_starts = nn_dot(below.astype(jnp.bfloat16), wide.astype(jnp.bfloat16))
+    starts_ref[...] = starts
+    ends_ref[...] = ends
+    row = iota((ROWS, 128), 0).astype(jnp.float32)
+    lane = iota((ROWS, 128), 1)
+
+    def one_hot(loader):
+        low = starts_ref[pl.ds(loader, 1), :]
+        high = ends_ref[pl.ds(loader, 1), :]
+        return jnp.where((row >= low) & (row < high), 1.0, 0.0)
+
+    heights = jnp.broadcast_to(dims_ref[0:1, :], (devices, devices)).astype(jnp.float32)
+    widths = jnp.broadcast_to(dims_ref[1:2, :], (devices, devices)).astype(jnp.float32)
+    spread = jnp.where(src == dst, 1.0, 0.0).astype(jnp.bfloat16)
+    before = jnp.where(src < dst, 1.0, 0.0).astype(jnp.bfloat16)
+    first_tile = nn_dot((heights * widths).astype(jnp.bfloat16), before)
+    widths = nn_dot(widths.astype(jnp.bfloat16), spread)
+    tile = src.astype(jnp.float32)
+    image = jnp.sum(jnp.where(first_tile <= tile, 1.0, 0.0), axis=1, keepdims=True) - 1.0
+    picked = jnp.where(dst.astype(jnp.float32) == image, 1.0, 0.0)
+    local = tile[:, 0:1] - jnp.sum(picked * first_tile, axis=1, keepdims=True)
+    across = jnp.maximum(jnp.sum(picked * widths, axis=1, keepdims=True), 1.0)
+    tile_row = jnp.floor((local + 0.5) / across)
+    tile_col = local - tile_row * across
+    places = jnp.where(dst == 0, tile_row * TR, jnp.where(dst == 1, tile_col * TC, 0.0))
+    picked_low = picked.astype(jnp.bfloat16)
+    same_image = nn_dot(nt_dot(picked_low, picked_low).astype(jnp.bfloat16), spread)
+
+    mine = one_hot(me)
+    own_row = iota((devices, 128), 0) == me
+    shift = jnp.sum(jnp.where(own_row, column_starts - starts, 0.0), axis=0, keepdims=True)
+    within = row[:, 0:1] + jnp.sum(mine * shift, axis=1, keepdims=True)
+    place = nn_dot(mine[:, 0:devices].astype(jnp.bfloat16), places.astype(jnp.bfloat16))
+    line = jnp.floor(within * (1.0 / TC))
+    row_pos = place[:, 0:1] + line
+    col_pos = place[:, 1:2] + within - line * TC
+    angle = jnp.where(lane < HD // 2, row_pos, col_pos) * freq_ref[0:1, :]
+    leading = (lane % (HD // 2)) < HD // 4
+    cosine = jnp.cos(angle)
+    sine = jnp.where(leading, -1.0, 1.0) * jnp.sin(angle)
+
+    def turn(values):
+        ahead = pltpu.roll(values, HD - HD // 4, 1)
+        behind = pltpu.roll(values, HD // 4, 1)
+        return (values * cosine + jnp.where(leading, ahead, behind) * sine).astype(jnp.bfloat16)
+
+    mask_row = jnp.concatenate(
+        [mask_ref[...].astype(jnp.float32), jnp.zeros((1, 128 - WIN), jnp.float32)], axis=1
+    )
+    extra = jnp.where(iota((EXTRA, 128), 0) == me, mask_row, 0.0).astype(jnp.bfloat16)
+    for h in range(H):
+        at = h * HD
+        q_out[h] = turn(qkv_ref[:, at : at + HD].astype(jnp.float32))
+        at = (H + h) * HD
+        k_out[h, 0:ROWS] = turn(qkv_ref[:, at : at + HD].astype(jnp.float32))
+        k_out[h, ROWS : ROWS + EXTRA] = extra
+
+    pl.semaphore_wait(barrier, chips)
+
+    def value_block(h):
+        return qkv_ref.at[:, pl.ds(pl.multiple_of((2 * H + h) * HD, HD), HD)]
+
+    def parcel(kind, h, loader, slot, target):
+        if kind == 0:
+            source, dest = k_out.at[h], k_in.at[loader]
+        elif kind == 1:
+            source, dest = q_out.at[h], q_in.at[slot]
+        else:
+            source, dest = value_block(h), v_in.at[loader]
+        return pltpu.make_async_remote_copy(
+            src_ref=source,
+            dst_ref=dest,
+            send_sem=send_sem.at[kind, h],
+            recv_sem=recv_sem.at[kind, slot],
+            device_id=device(target),
+            device_id_type=MESH_ID,
+        )
+
+    def relay(kind, slot):
+        ref = k_in if kind == 0 else v_in
+        block = ref.at[slot * 2 + core]
+        return pltpu.make_async_remote_copy(
+            src_ref=block,
+            dst_ref=block,
+            send_sem=pass_send_sem.at[kind, slot],
+            recv_sem=pass_recv_sem.at[kind, slot],
+            device_id=device(sibling),
+            device_id_type=MESH_ID,
+        )
+
+    def relayed(kind, slot):
+        ref = k_in if kind == 0 else v_in
+        block = ref.at[slot * 2 + 1 - core]
+        return pltpu.make_async_remote_copy(
+            src_ref=block,
+            dst_ref=block,
+            send_sem=pass_send_sem.at[kind, slot],
+            recv_sem=pass_recv_sem.at[kind, slot],
+            device_id=device(sibling),
+            device_id_type=MESH_ID,
+        )
+
+    def back(h, slot, target):
+        return pltpu.make_async_remote_copy(
+            src_ref=done_ref.at[slot],
+            dst_ref=home_ref.at[h],
+            send_sem=back_send_sem.at[slot],
+            recv_sem=back_recv_sem.at[h],
+            device_id=device(target),
+            device_id_type=MESH_ID,
+        )
+
+    def each_target(action):
+        for kind in range(3):
+            for hop in range(1, chips):
+                to_chip = chip ^ hop
+                h = to_chip - first_chip
+
+                @pl.when((h >= 0) & (h < H))
+                def _():
+                    action(parcel(kind, h, me, chip, to_chip * 2 + core))
+
+    each_target(lambda copy: copy.start())
+
+    @pl.when(has_head)
+    def _():
+        k_in[me] = k_out[head]
+        q_in[chip] = q_out[head]
+        v_in[me] = qkv_ref[:, pl.ds(pl.multiple_of((2 * H + head) * HD, HD), HD)]
+        relay(0, chip).start()
+        relay(2, chip).start()
+
+        def make_tiles(loader, carry):
+            tile_of[loader] = one_hot(loader).astype(jnp.bfloat16)
+            return carry
+
+        lax.fori_loop(0, devices, make_tiles, 0)
+        for hop in range(1, chips):
+            slot = chip ^ hop
+            parcel(0, head, slot * 2 + core, slot, me).wait_recv()
+            relay(0, slot).start()
+        for hop in range(chips):
+            relayed(0, chip ^ hop).wait_recv()
+
+        bits = jnp.sum(k_in[:, ROWS : ROWS + EXTRA, :].astype(jnp.float32), axis=0)
+        seen = jnp.zeros((EXTRA, 128), jnp.float32)
+        apart = iota((EXTRA, 128), 1) - iota((EXTRA, 128), 0) + (MAXT - 1)
+        for o in range(WIN):
+            seen = seen + jnp.where(apart == o, bits[:, o : o + 1], 0.0)
+        allowed = (seen > 0.5) & (same_image > 0.5)
+        hidden = jnp.where(allowed, 0.0, HIDDEN).astype(jnp.bfloat16)
+        bias_ref[...] = hidden
+
+        factor = math.log2(math.e) / math.sqrt(HD)
+
+        def score(hop, carry):
+            slot = chip ^ hop
+
+            @pl.when(hop > 0)
+            def _():
+                parcel(1, head, slot * 2 + core, slot, me).wait_recv()
+
+            own_tile = tile_of[slot * 2 + core][:, 0:EXTRA]
+            veil = nn_dot(own_tile, bias_ref[...]).astype(jnp.bfloat16)
+            query = jnp.concatenate([q_in[slot], veil], axis=1)
+            key = jnp.concatenate(
+                [
+                    k_in[:, 0:ROWS, :].reshape(devices * ROWS, HD),
+                    tile_of[...].reshape(devices * ROWS, 128),
+                ],
+                axis=1,
+            )
+            scores = nt_dot(query, key)
+            top = jnp.max(scores, axis=1, keepdims=True)
+            weight = jnp.exp2((scores - top) * factor)
+            sum_ref[slot] = jnp.broadcast_to(jnp.sum(weight, axis=1, keepdims=True), (ROWS, 128))
+            weight = weight.astype(jnp.bfloat16)
+            for c in range(chips):
+                weights_ref[c, pl.ds(pl.multiple_of(slot * ROWS, ROWS), ROWS), :] = weight[
+                    :, c * 2 * ROWS : (c + 1) * 2 * ROWS
+                ]
+            return carry
+
+        lax.fori_loop(0, chips, score, 0)
+
+        for hop in range(1, chips):
+            slot = chip ^ hop
+            parcel(2, head, slot * 2 + core, slot, me).wait_recv()
+            relay(2, slot).start()
+
+        total_ref[...] = jnp.zeros_like(total_ref)
+
+        def mix(hop, carry):
+            slot = chip ^ hop
+            relayed(2, slot).wait_recv()
+            value = v_in[pl.ds(slot * 2, 2)].reshape(2 * ROWS, HD)
+            total_ref[...] += nn_dot(weights_ref[slot], value)
+            return carry
+
+        lax.fori_loop(0, chips, mix, 0)
+
+        for hop in range(chips - 1, -1, -1):
+            slot = chip ^ hop
+            rows = pl.ds(pl.multiple_of(slot * ROWS, ROWS), ROWS)
+            done_ref[slot] = (total_ref[rows, :] / sum_ref[slot]).astype(jnp.bfloat16)
+            if hop:
+                back(head, slot, slot * 2 + core).start()
+            else:
+                home_ref[head] = done_ref[slot]
+
+        for hop in range(chips):
+            relay(0, chip ^ hop).wait_send()
+            relay(2, chip ^ hop).wait_send()
+            if hop:
+                back(head, chip ^ hop, (chip ^ hop) * 2 + core).wait_send()
+
+    each_target(lambda copy: copy.wait_send())
+    for h in range(H):
+
+        @pl.when(head != h)
+        def _():
+            back(h, chip, me).wait_recv()
+
+        out_ref[:, h * HD : (h + 1) * HD] = home_ref[h]
+
+
+def by_head(qkv_rows, pair_counts, image_dims, block_mask, out_weight):
+    devices = lax.axis_size("inner")
+    chips = devices // 2
+    low = jnp.bfloat16
+    quarter = HD // 4
+    lane = np.arange(HD) % quarter
+    frequency = np.power(np.float32(10000.0), -lane.astype(np.float32) / np.float32(quarter))
+    frequency = np.broadcast_to(frequency.astype(np.float32), (8, HD))
+    attended = pl.pallas_call(
+        functools.partial(head_kernel, devices),
+        name="attend",
+        out_shape=jax.ShapeDtypeStruct((ROWS, H * HD), low),
+        in_specs=[pl.BlockSpec(memory_space=pltpu.VMEM)] * 5,
+        out_specs=pl.BlockSpec(memory_space=pltpu.VMEM),
+        scratch_shapes=[
+            pltpu.VMEM((H, ROWS, HD), low),
+            pltpu.VMEM((H, ROWS + EXTRA, HD), low),
+            pltpu.VMEM((chips, ROWS, HD), low),
+            pltpu.VMEM((devices, ROWS + EXTRA, HD), low),
+            pltpu.VMEM((devices, ROWS, HD), low),
+            pltpu.VMEM((devices, ROWS, 128), low),
+            pltpu.VMEM((devices, 128), jnp.float32),
+            pltpu.VMEM((devices, 128), jnp.float32),
+            pltpu.VMEM((EXTRA, 128), low),
+            pltpu.VMEM((chips, chips * ROWS, 2 * ROWS), low),
+            pltpu.VMEM((chips, ROWS, 128), jnp.float32),
+            pltpu.VMEM((chips * ROWS, HD), jnp.float32),
+            pltpu.VMEM((chips, ROWS, HD), low),
+            pltpu.VMEM((H, ROWS, HD), low),
+            pltpu.SemaphoreType.DMA((3, H)),
+            pltpu.SemaphoreType.DMA((3, chips)),
+            pltpu.SemaphoreType.DMA((3, chips)),
+            pltpu.SemaphoreType.DMA((3, chips)),
+            pltpu.SemaphoreType.DMA((chips,)),
+            pltpu.SemaphoreType.DMA((H,)),
+        ],
+        compiler_params=pltpu.CompilerParams(
+            collective_id=0, has_side_effects=True, vmem_limit_bytes=48 * 1024 * 1024
+        ),
+        cost_estimate=pl.CostEstimate(
+            flops=2 * 1024 * 2048 * 384, bytes_accessed=1 << 20, transcendentals=1024 * 2048
+        ),
+    )(qkv_rows, pair_counts, image_dims, block_mask, jnp.asarray(frequency))
+    return jnp.dot(attended, out_weight, preferred_element_type=jnp.float32).astype(low)
+
+
 def solution(mesh):
+    body = by_head if mesh.shape["inner"] == EXTRA else shards
     in_specs = (
         P(("group", "inner"), None),
         P("group", None),
@@ -172,4 +528,4 @@
         P(),
     )
     out_specs = P(("group", "inner"), None)
-    return jax.shard_map(shards, mesh=mesh, in_specs=in_specs, out_specs=out_specs, check_vma=False)
+    return jax.shard_map(body, mesh=mesh, in_specs=in_specs, out_specs=out_specs, check_vma=False)

time: 165 us -> 38.1 us (0.23)
  waiting for transfers between devices: 79.8 us -> 0 us
  Pallas kernels: 0 us -> 32.7 us
  other arithmetic: 27.2 us -> 0 us
  local copies, waits for them, and re-layouts: 21.9 us -> 3.9 us
  starting transfers between devices: 17 us -> 0 us
  loops' own time: 7.9 us -> 0 us
  matrix products: 7.07 us -> 1.23 us
  between operations: 3.55 us -> 0.02 us
    ppermute x7 -> x0, waiting for transfers between devices: 48.6 us -> none  [from_behind(): return lax.ppermute(value, axis, pairs)]
    pallas_call x0 -> x1, Pallas kernels: none -> 32.7 us  [by_head(): pl.pallas_call(functools.partial(head_kernel, devices), name='attend', ou...]
    all_to_all x2 -> x0, waiting for transfers between devices: 31.2 us -> none  [the longest x1 18.4 us: shards(): lax.all_to_all(returning, 'inner', split_axis=0, concat_axis=0, tiled=True)]
    all_to_all x2 -> x0, starting transfers between devices: 11.3 us -> none  [the longest x1 7.52 us: shards(): lax.all_to_all(parcels, 'inner', split_axis=0, concat_axis=0, tiled=True)]
    select_n x14 -> x0, other arithmetic: 8.65 us -> none  [the longest x6 3.71 us: visit(): jnp.take_along_axis(block_mask, jnp.clip(offset, 0, WIN - 1), axis=1)]
    gather x5 -> x0, local copies, waits for them, and re-layouts: 8.39 us -> none  [the longest x1 3.72 us: shards(): jnp.take(qkv_rows, outgoing, axis=0)]
    reduce_sum x20 -> x0, other arithmetic: 8.13 us -> none  [the longest x8 5.9 us: block_places(): image_id = jnp.sum(inside, axis=1) - 1]
    another operation x1 -> x0, loops' own time: 7.9 us -> none  [shards(): lax.fori_loop(0, 2 * reach_count, one_way, (farthest, softmax_state))[1]]
  transfers between devices with their start and end apart: 9 -> 0, of which waited for: 9 -> 0; matrix products, arithmetic and copies ran while one was open for 12% -> 0% of each run, Pallas kernels for 0% -> 0%
where the time goes in v1:
time: 38.1 us; the launch traced here: 37.9 us
  Pallas kernels  32.7 us (86%)
  local copies, waits for them, and re-layouts  3.9 us (10%)
  matrix products  1.23 us (3%)
    pallas_call x1, Pallas kernels, by_head(): pl.pallas_call(functools.partial(head_kernel, devices), name='attend', ou...  32.7 us
    unnamed x10, local copies, waits for them, and re-layouts  3.1 us
    dot_general x1, matrix products, by_head(): jnp.dot(attended, out_weight, preferred_element_type=jnp.float32)  1.23 us
    another operation x1, local copies, waits for them, and re-layouts  0.81 us

profile of v1, /device:TPU:0, one launch (start us, length us, event | category | flops | bytes accessed | tf_op | source)
XLA Modules:
  0.0 37.9 jit_solution(18167194087345843833)
XLA Ops:
  0.0 0.0 copy-start
  0.0 0.8 %jit_solution_.3.freq_ref = f32[8,128]{1,0:T(8,128)S(1)} broadcast(f32[128]{0:T(128)} %constant.2.clone), dimensions={1} | broadcast | bytes 4608 | tf_op jit(solution)
  0.8 0.0 copy-start.1
  0.8 1.1 %copy-done.1 = bf16[128,2304]{1,0:T(8,128)(2,1)S(1)} copy-done((bf16[128,2304]{1,0:T(8,128)(2,1)S(1)}, bf16[128,2304]{1,0:T(8,128)(2,1)}, u32[]{:S(2)}) %copy-start.1) | copy-done | bytes 589848
  1.9 0.0 copy-start.2
  1.9 0.7 %copy-done.2 = s32[16,16]{1,0:T(8,128)S(1)} copy-done((s32[16,16]{1,0:T(8,128)S(1)}, s32[16,16]{1,0:T(8,128)}, u32[]{:S(2)}) %copy-start.2) | copy-done | bytes 1048
  2.6 0.0 copy-start.3
  2.6 0.7 %copy-done.3 = s32[2,16]{1,0:T(2,128)S(1)} copy-done((s32[2,16]{1,0:T(2,128)S(1)}, s32[2,16]{1,0:T(2,128)}, u32[]{:S(2)}) %copy-start.3) | copy-done | bytes 152
  3.3 0.0 copy-start.4
  3.3 0.7 %copy-done.4 = s32[1,7]{1,0:T(1,128)S(1)} copy-done((s32[1,7]{1,0:T(1,128)S(1)}, s32[1,7]{1,0:T(1,128)}, u32[]{:S(2)}) %copy-start.4) | copy-done | bytes 52
  3.9 32.7 %attend.1 = bf16[128,768]{1,0:T(8,128)(2,1)S(1)} custom-call(bf16[128,2304]{1,0:T(8,128)(2,1)S(1)} %copy-done.1, s32[16,16]{1,0:T(8,128)S(1)} %copy-done.2, s32[2,16]{1,0:T(2,128)S(1)} %copy-done.3, s32[1,7]{1,0:T(1,128)S(1)} %copy-done.4, f32[8,128]{1,0:T(8,128)S(1)} %jit_solution_.3.freq_ref), custom_call_target="tpu_custom_call" | custom-call | flops 1610612736 | bytes 1048576 | tf_op jit(solution)/shard_map/attend/pallas_call | solution.py:483
  36.6 0.0 copy-done
  36.6 1.2 %convolution_convert_fusion = bf16[128,1536]{1,0:T(8,128)(2,1)} fusion(bf16[128,768]{1,0:T(8,128)(2,1)S(1)} %attend.1, bf16[768,1536]{1,0:T(8,128)(2,1)S(1)} %copy-done), kind=kOutput, calls=%fused_computation | convolution fusion | flops 302186496 | bytes 2949120 | tf_op jit(solution)/shard_map/dot_general | solution.py:518
Async XLA Ops:
  0.0 36.6 %copy-start = (bf16[768,1536]{1,0:T(8,128)(2,1)S(1)}, bf16[768,1536]{1,0:T(8,128)(2,1)}, u32[]{:S(2)}) copy-start(bf16[768,1536]{1,0:T(8,128)(2,1)} %param.10) | copy-start | bytes 7077892
  0.8 1.1 %copy-start.1 = (bf16[128,2304]{1,0:T(8,128)(2,1)S(1)}, bf16[128,2304]{1,0:T(8,128)(2,1)}, u32[]{:S(2)}) copy-start(bf16[128,2304]{1,0:T(8,128)(2,1)} %qkv_ref.1) | copy-start | bytes 1769476
  1.9 0.7 %copy-start.2 = (s32[16,16]{1,0:T(8,128)S(1)}, s32[16,16]{1,0:T(8,128)}, u32[]{:S(2)}) copy-start(s32[16,16]{1,0:T(8,128)} %pair_ref.1) | copy-start | bytes 3076
  2.6 0.7 %copy-start.3 = (s32[2,16]{1,0:T(2,128)S(1)}, s32[2,16]{1,0:T(2,128)}, u32[]{:S(2)}) copy-start(s32[2,16]{1,0:T(2,128)} %dims_ref.1) | copy-start | bytes 388
  3.3 0.7 %copy-start.4 = (s32[1,7]{1,0:T(1,128)S(1)}, s32[1,7]{1,0:T(1,128)}, u32[]{:S(2)}) copy-start(s32[1,7]{1,0:T(1,128)} %mask_ref.1) | copy-start | bytes 88

commit v2 on v1

--- a/solution.py
+++ b/solution.py
@@ -3,7 +3,6 @@
 
 import jax
 import jax.numpy as jnp
-import numpy as np
 from jax import lax
 from jax.experimental import pallas as pl
 from jax.experimental.pallas import tpu as pltpu
@@ -192,14 +191,19 @@
 
 def head_kernel(
     devices,
+    qkv_hbm,
+    pair_hbm,
+    dims_hbm,
+    mask_hbm,
+    out_ref,
     qkv_ref,
     pair_ref,
     dims_ref,
     mask_ref,
-    freq_ref,
-    out_ref,
+    load_sem,
     q_out,
     k_out,
+    v_out,
     q_in,
     k_in,
     v_in,
@@ -207,9 +211,6 @@
     starts_ref,
     ends_ref,
     bias_ref,
-    weights_ref,
-    sum_ref,
-    total_ref,
     done_ref,
     home_ref,
     send_sem,
@@ -239,6 +240,44 @@
         )
     pl.semaphore_signal(barrier, inc=1, device_id=device(sibling), device_id_type=MESH_ID)
 
+    inner_width = H * HD
+
+    def load(source, dest, index):
+        copy = pltpu.make_async_copy(source, dest, load_sem.at[index])
+        copy.start()
+        return copy
+
+    def columns(part):
+        at = part * inner_width
+        return qkv_hbm.at[:, at : at + inner_width], qkv_ref.at[:, at : at + inner_width]
+
+    load_pair = load(pair_hbm, pair_ref, 0)
+    load_dims = load(dims_hbm, dims_ref, 1)
+    load_mask = load(mask_hbm, mask_ref, 2)
+    load_key = load(*columns(1), 3)
+    load_value = load(*columns(2), 4)
+    load_query = load(*columns(0), 5)
+
+    row = iota((ROWS, 128), 0).astype(jnp.float32)
+    lane = iota((ROWS, 128), 1)
+    quarter = HD // 4
+    half = HD // 2
+    power = (lane % quarter).astype(jnp.float32) * (-math.log(10000.0) / quarter)
+    upper = iota((ROWS, 128), 0) < half
+    angle = jnp.where(upper, row, row - half) * jnp.exp(power)
+    leading = (lane % half) < quarter
+    paired = upper == (lane < half)
+    cosine_table = jnp.where(paired, jnp.cos(angle), 0.0)
+    sine_table = jnp.where(paired, jnp.where(leading, -1.0, 1.0) * jnp.sin(angle), 0.0)
+    table = jnp.concatenate([cosine_table, sine_table], axis=1)
+    high_part = table.astype(jnp.bfloat16)
+    left_over = table - high_part.astype(jnp.float32)
+    mid_part = left_over.astype(jnp.bfloat16)
+    low_part = (left_over - mid_part.astype(jnp.float32)).astype(jnp.bfloat16)
+    load_pair.wait()
+    load_dims.wait()
+    load_mask.wait()
+
     src = iota((devices, 128), 0)
     dst = iota((devices, 128), 1)
     pairs = pair_ref[...].astype(jnp.float32).astype(jnp.bfloat16)
@@ -249,8 +288,6 @@
     column_starts = nn_dot(below.astype(jnp.bfloat16), wide.astype(jnp.bfloat16))
     starts_ref[...] = starts
     ends_ref[...] = ends
-    row = iota((ROWS, 128), 0).astype(jnp.float32)
-    lane = iota((ROWS, 128), 1)
 
     def one_hot(loader):
         low = starts_ref[pl.ds(loader, 1), :]
@@ -282,10 +319,12 @@
     line = jnp.floor(within * (1.0 / TC))
     row_pos = place[:, 0:1] + line
     col_pos = place[:, 1:2] + within - line * TC
-    angle = jnp.where(lane < HD // 2, row_pos, col_pos) * freq_ref[0:1, :]
-    leading = (lane % (HD // 2)) < HD // 4
-    cosine = jnp.cos(angle)
-    sine = jnp.where(leading, -1.0, 1.0) * jnp.sin(angle)
+    lane_at = lane.astype(jnp.float32)
+    chosen = (lane_at == row_pos) | (lane_at == col_pos + half)
+    chosen = jnp.where(chosen, 1.0, 0.0).astype(jnp.bfloat16)
+    circle = nn_dot(chosen, high_part) + (nn_dot(chosen, mid_part) + nn_dot(chosen, low_part))
+    cosine = circle[:, 0:HD]
+    sine = circle[:, HD : 2 * HD]
 
     def turn(values):
         ahead = pltpu.roll(values, HD - HD // 4, 1)
@@ -296,17 +335,13 @@
         [mask_ref[...].astype(jnp.float32), jnp.zeros((1, 128 - WIN), jnp.float32)], axis=1
     )
     extra = jnp.where(iota((EXTRA, 128), 0) == me, mask_row, 0.0).astype(jnp.bfloat16)
+    load_key.wait()
     for h in range(H):
-        at = h * HD
-        q_out[h] = turn(qkv_ref[:, at : at + HD].astype(jnp.float32))
         at = (H + h) * HD
         k_out[h, 0:ROWS] = turn(qkv_ref[:, at : at + HD].astype(jnp.float32))
         k_out[h, ROWS : ROWS + EXTRA] = extra
 
     pl.semaphore_wait(barrier, chips)
-
-    def value_block(h):
-        return qkv_ref.at[:, pl.ds(pl.multiple_of((2 * H + h) * HD, HD), HD)]
 
     def parcel(kind, h, loader, slot, target):
         if kind == 0:
@@ -314,7 +349,7 @@
         elif kind == 1:
             source, dest = q_out.at[h], q_in.at[slot]
         else:
-            source, dest = value_block(h), v_in.at[loader]
+            source, dest = v_out.at[h], v_in.at[loader]
         return pltpu.make_async_remote_copy(
             src_ref=source,
             dst_ref=dest,
@@ -358,25 +393,42 @@
             device_id_type=MESH_ID,
         )
 
-    def each_target(action):
-        for kind in range(3):
-            for hop in range(1, chips):
-                to_chip = chip ^ hop
-                h = to_chip - first_chip
-
-                @pl.when((h >= 0) & (h < H))
-                def _():
-                    action(parcel(kind, h, me, chip, to_chip * 2 + core))
-
-    each_target(lambda copy: copy.start())
+    def each_target(kind, action):
+        for hop in range(chips - 1, 0, -1):
+            to_chip = chip ^ hop
+            h = to_chip - first_chip
+
+            @pl.when((h >= 0) & (h < H))
+            def _():
+                action(parcel(kind, h, me, chip, to_chip * 2 + core))
+
+    each_target(0, lambda copy: copy.start())
 
     @pl.when(has_head)
     def _():
         k_in[me] = k_out[head]
+        relay(0, chip).start()
+
+    load_value.wait()
+    for h in range(H):
+        at = (2 * H + h) * HD
+        v_out[h] = qkv_ref[:, at : at + HD].T
+    each_target(2, lambda copy: copy.start())
+
+    @pl.when(has_head)
+    def _():
+        v_in[me] = v_out[head]
+        relay(2, chip).start()
+
+    load_query.wait()
+    for h in range(H):
+        at = h * HD
+        q_out[h] = turn(qkv_ref[:, at : at + HD].astype(jnp.float32))
+    each_target(1, lambda copy: copy.start())
+
+    @pl.when(has_head)
+    def _():
         q_in[chip] = q_out[head]
-        v_in[me] = qkv_ref[:, pl.ds(pl.multiple_of((2 * H + head) * HD, HD), HD)]
-        relay(0, chip).start()
-        relay(2, chip).start()
 
         def make_tiles(loader, carry):
             tile_of[loader] = one_hot(loader).astype(jnp.bfloat16)
@@ -387,8 +439,14 @@
             slot = chip ^ hop
             parcel(0, head, slot * 2 + core, slot, me).wait_recv()
             relay(0, slot).start()
+        for hop in range(1, chips):
+            slot = chip ^ hop
+            parcel(2, head, slot * 2 + core, slot, me).wait_recv()
+            relay(2, slot).start()
         for hop in range(chips):
             relayed(0, chip ^ hop).wait_recv()
+        for hop in range(chips):
+            relayed(2, chip ^ hop).wait_recv()
 
         bits = jnp.sum(k_in[:, ROWS : ROWS + EXTRA, :].astype(jnp.float32), axis=0)
         seen = jnp.zeros((EXTRA, 128), jnp.float32)
@@ -418,43 +476,22 @@
                 ],
                 axis=1,
             )
-            scores = nt_dot(query, key)
-            top = jnp.max(scores, axis=1, keepdims=True)
+            scores = nt_dot(key, query)
+            top = jnp.max(scores, axis=0, keepdims=True)
             weight = jnp.exp2((scores - top) * factor)
-            sum_ref[slot] = jnp.broadcast_to(jnp.sum(weight, axis=1, keepdims=True), (ROWS, 128))
-            weight = weight.astype(jnp.bfloat16)
-            for c in range(chips):
-                weights_ref[c, pl.ds(pl.multiple_of(slot * ROWS, ROWS), ROWS), :] = weight[
-                    :, c * 2 * ROWS : (c + 1) * 2 * ROWS
-                ]
+            row_sum = jnp.sum(weight, axis=0, keepdims=True)
+            value = jnp.concatenate([v_in[d] for d in range(devices)], axis=1)
+            mixed = nn_dot(value, weight.astype(jnp.bfloat16)) / row_sum
+            done_ref[slot] = mixed.T.astype(jnp.bfloat16)
+
+            @pl.when(hop > 0)
+            def _():
+                back(head, slot, slot * 2 + core).start()
+
             return carry
 
         lax.fori_loop(0, chips, score, 0)
-
-        for hop in range(1, chips):
-            slot = chip ^ hop
-            parcel(2, head, slot * 2 + core, slot, me).wait_recv()
-            relay(2, slot).start()
-
-        total_ref[...] = jnp.zeros_like(total_ref)
-
-        def mix(hop, carry):
-            slot = chip ^ hop
-            relayed(2, slot).wait_recv()
-            value = v_in[pl.ds(slot * 2, 2)].reshape(2 * ROWS, HD)
-            total_ref[...] += nn_dot(weights_ref[slot], value)
-            return carry
-
-        lax.fori_loop(0, chips, mix, 0)
-
-        for hop in range(chips - 1, -1, -1):
-            slot = chip ^ hop
-            rows = pl.ds(pl.multiple_of(slot * ROWS, ROWS), ROWS)
-            done_ref[slot] = (total_ref[rows, :] / sum_ref[slot]).astype(jnp.bfloat16)
-            if hop:
-                back(head, slot, slot * 2 + core).start()
-            else:
-                home_ref[head] = done_ref[slot]
+        home_ref[head] = done_ref[chip]
 
         for hop in range(chips):
             relay(0, chip ^ hop).wait_send()
@@ -462,7 +499,8 @@
             if hop:
                 back(head, chip ^ hop, (chip ^ hop) * 2 + core).wait_send()
 
-    each_target(lambda copy: copy.wait_send())
+    for kind in range(3):
+        each_target(kind, lambda copy: copy.wait_send())
     for h in range(H):
 
         @pl.when(head != h)
@@ -476,19 +514,21 @@
     devices = lax.axis_size("inner")
     chips = devices // 2
     low = jnp.bfloat16
-    quarter = HD // 4
-    lane = np.arange(HD) % quarter
-    frequency = np.power(np.float32(10000.0), -lane.astype(np.float32) / np.float32(quarter))
-    frequency = np.broadcast_to(frequency.astype(np.float32), (8, HD))
     attended = pl.pallas_call(
         functools.partial(head_kernel, devices),
         name="attend",
         out_shape=jax.ShapeDtypeStruct((ROWS, H * HD), low),
-        in_specs=[pl.BlockSpec(memory_space=pltpu.VMEM)] * 5,
+        in_specs=[pl.BlockSpec(memory_space=pltpu.HBM)] * 4,
         out_specs=pl.BlockSpec(memory_space=pltpu.VMEM),
         scratch_shapes=[
+            pltpu.VMEM(qkv_rows.shape, low),
+            pltpu.VMEM(pair_counts.shape, jnp.int32),
+            pltpu.VMEM(image_dims.shape, jnp.int32),
+            pltpu.VMEM(block_mask.shape, jnp.int32),
+            pltpu.SemaphoreType.DMA((6,)),
             pltpu.VMEM((H, ROWS, HD), low),
             pltpu.VMEM((H, ROWS + EXTRA, HD), low),
+            pltpu.VMEM((H, HD, ROWS), low),
             pltpu.VMEM((chips, ROWS, HD), low),
             pltpu.VMEM((devices, ROWS + EXTRA, HD), low),
             pltpu.VMEM((devices, ROWS, HD), low),
@@ -496,9 +536,6 @@
             pltpu.VMEM((devices, 128), jnp.float32),
             pltpu.VMEM((devices, 128), jnp.float32),
             pltpu.VMEM((EXTRA, 128), low),
-            pltpu.VMEM((chips, chips * ROWS, 2 * ROWS), low),
-            pltpu.VMEM((chips, ROWS, 128), jnp.float32),
-            pltpu.VMEM((chips * ROWS, HD), jnp.float32),
             pltpu.VMEM((chips, ROWS, HD), low),
             pltpu.VMEM((H, ROWS, HD), low),
             pltpu.SemaphoreType.DMA((3, H)),
@@ -514,7 +551,7 @@
         cost_estimate=pl.CostEstimate(
             flops=2 * 1024 * 2048 * 384, bytes_accessed=1 << 20, transcendentals=1024 * 2048
         ),
-    )(qkv_rows, pair_counts, image_dims, block_mask, jnp.asarray(frequency))
+    )(qkv_rows, pair_counts, image_dims, block_mask)
     return jnp.dot(attended, out_weight, preferred_element_type=jnp.float32).astype(low)
 
 

time: 38.1 us -> 37.9 us (level)
  local copies, waits for them, and re-layouts: 3.9 us -> 3.25 us
    another operation x1 -> x0, local copies, waits for them, and re-layouts: 0.81 us -> none
where the time goes in v2:
time: 37.9 us; the launch traced here: 37.4 us
  Pallas kernels  32.9 us (87%)
  local copies, waits for them, and re-layouts  3.25 us (9%)
  matrix products  1.23 us (3%)
    pallas_call x1, Pallas kernels, by_head(): pl.pallas_call(functools.partial(head_kernel, devices), name='attend', ou...  32.9 us
    unnamed x10, local copies, waits for them, and re-layouts  3.25 us
    dot_general x1, matrix products, by_head(): jnp.dot(attended, out_weight, preferred_element_type=jnp.float32)  1.23 us

profile of v2, /device:TPU:0, one launch (start us, length us, event | category | flops | bytes accessed | tf_op | source)
XLA Modules:
  0.0 37.4 jit_solution(11321633667827957054)
XLA Ops:
  0.0 0.0 copy-start
  0.0 0.0 copy-start.1
  0.0 1.2 %copy-done.1 = bf16[128,2304]{1,0:T(8,128)(2,1)S(1)} copy-done((bf16[128,2304]{1,0:T(8,128)(2,1)S(1)}, bf16[128,2304]{1,0:T(8,128)(2,1)}, u32[]{:S(2)}) %copy-start.1) | copy-done | bytes 589848
  1.2 0.0 copy-start.2
  1.2 0.7 %copy-done.2 = s32[16,16]{1,0:T(8,128)S(1)} copy-done((s32[16,16]{1,0:T(8,128)S(1)}, s32[16,16]{1,0:T(8,128)}, u32[]{:S(2)}) %copy-start.2) | copy-done | bytes 1048
  1.9 0.0 copy-start.3
  1.9 0.7 %copy-done.3 = s32[2,16]{1,0:T(2,128)S(1)} copy-done((s32[2,16]{1,0:T(2,128)S(1)}, s32[2,16]{1,0:T(2,128)}, u32[]{:S(2)}) %copy-start.3) | copy-done | bytes 152
  2.6 0.0 copy-start.4
  2.6 0.7 %copy-done.4 = s32[1,7]{1,0:T(1,128)S(1)} copy-done((s32[1,7]{1,0:T(1,128)S(1)}, s32[1,7]{1,0:T(1,128)}, u32[]{:S(2)}) %copy-start.4) | copy-done | bytes 52
  3.3 32.9 %attend.1 = bf16[128,768]{1,0:T(8,128)(2,1)S(1)} custom-call(bf16[128,2304]{1,0:T(8,128)(2,1)S(1)} %copy-done.1, s32[16,16]{1,0:T(8,128)S(1)} %copy-done.2, s32[2,16]{1,0:T(2,128)S(1)} %copy-done.3, s32[1,7]{1,0:T(1,128)S(1)} %copy-done.4), custom_call_target="tpu_custom_call" | custom-call | flops 1610612736 | bytes 1048576 | tf_op jit(solution)/shard_map/attend/pallas_call | solution.py:517
  36.1 0.0 copy-done
  36.1 1.2 %convolution_convert_fusion = bf16[128,1536]{1,0:T(8,128)(2,1)} fusion(bf16[128,768]{1,0:T(8,128)(2,1)S(1)} %attend.1, bf16[768,1536]{1,0:T(8,128)(2,1)S(1)} %copy-done), kind=kOutput, calls=%fused_computation | convolution fusion | flops 302186496 | bytes 2949120 | tf_op jit(solution)/shard_map/dot_general | solution.py:555
Async XLA Ops:
  0.0 36.1 %copy-start = (bf16[768,1536]{1,0:T(8,128)(2,1)S(1)}, bf16[768,1536]{1,0:T(8,128)(2,1)}, u32[]{:S(2)}) copy-start(bf16[768,1536]{1,0:T(8,128)(2,1)} %param.9) | copy-start | bytes 7077892
  0.0 1.2 %copy-start.1 = (bf16[128,2304]{1,0:T(8,128)(2,1)S(1)}, bf16[128,2304]{1,0:T(8,128)(2,1)}, u32[]{:S(2)}) copy-start(bf16[128,2304]{1,0:T(8,128)(2,1)} %qkv_hbm.1) | copy-start | bytes 1769476
  1.2 0.7 %copy-start.2 = (s32[16,16]{1,0:T(8,128)S(1)}, s32[16,16]{1,0:T(8,128)}, u32[]{:S(2)}) copy-start(s32[16,16]{1,0:T(8,128)} %pair_hbm.1) | copy-start | bytes 3076
  1.9 0.7 %copy-start.3 = (s32[2,16]{1,0:T(2,128)S(1)}, s32[2,16]{1,0:T(2,128)}, u32[]{:S(2)}) copy-start(s32[2,16]{1,0:T(2,128)} %dims_hbm.1) | copy-start | bytes 388
  2.6 0.7 %copy-start.4 = (s32[1,7]{1,0:T(1,128)S(1)}, s32[1,7]{1,0:T(1,128)}, u32[]{:S(2)}) copy-start(s32[1,7]{1,0:T(1,128)} %mask_hbm.1) | copy-start | bytes 88

commit v3 on v2

--- a/solution.py
+++ b/solution.py
@@ -394,7 +394,7 @@
         )
 
     def each_target(kind, action):
-        for hop in range(chips - 1, 0, -1):
+        for hop in range(1, chips):
             to_chip = chip ^ hop
             h = to_chip - first_chip
 
@@ -459,16 +459,17 @@
 
         factor = math.log2(math.e) / math.sqrt(HD)
 
-        def score(hop, carry):
-            slot = chip ^ hop
-
-            @pl.when(hop > 0)
+        def score(turn_id, carry):
+            slots = [chip ^ (2 * turn_id), chip ^ (2 * turn_id + 1)]
+
+            @pl.when(turn_id > 0)
             def _():
-                parcel(1, head, slot * 2 + core, slot, me).wait_recv()
-
-            own_tile = tile_of[slot * 2 + core][:, 0:EXTRA]
-            veil = nn_dot(own_tile, bias_ref[...]).astype(jnp.bfloat16)
-            query = jnp.concatenate([q_in[slot], veil], axis=1)
+                parcel(1, head, slots[0] * 2 + core, slots[0], me).wait_recv()
+
+            parcel(1, head, slots[1] * 2 + core, slots[1], me).wait_recv()
+            own_tiles = jnp.concatenate([tile_of[d * 2 + core][:, 0:EXTRA] for d in slots], axis=0)
+            veil = nn_dot(own_tiles, bias_ref[...]).astype(jnp.bfloat16)
+            query = jnp.concatenate([jnp.concatenate([q_in[d] for d in slots], axis=0), veil], axis=1)
             key = jnp.concatenate(
                 [
                     k_in[:, 0:ROWS, :].reshape(devices * ROWS, HD),
@@ -482,15 +483,17 @@
             row_sum = jnp.sum(weight, axis=0, keepdims=True)
             value = jnp.concatenate([v_in[d] for d in range(devices)], axis=1)
             mixed = nn_dot(value, weight.astype(jnp.bfloat16)) / row_sum
-            done_ref[slot] = mixed.T.astype(jnp.bfloat16)
-
-            @pl.when(hop > 0)
+            done_ref[slots[0]] = mixed[:, 0:ROWS].T.astype(jnp.bfloat16)
+            done_ref[slots[1]] = mixed[:, ROWS : 2 * ROWS].T.astype(jnp.bfloat16)
+
+            @pl.when(turn_id > 0)
             def _():
-                back(head, slot, slot * 2 + core).start()
-
+                back(head, slots[0], slots[0] * 2 + core).start()
+
+            back(head, slots[1], slots[1] * 2 + core).start()
             return carry
 
-        lax.fori_loop(0, chips, score, 0)
+        lax.fori_loop(0, chips // 2, score, 0)
         home_ref[head] = done_ref[chip]
 
         for hop in range(chips):
@@ -546,7 +549,7 @@
             pltpu.SemaphoreType.DMA((H,)),
         ],
         compiler_params=pltpu.CompilerParams(
-            collective_id=0, has_side_effects=True, vmem_limit_bytes=48 * 1024 * 1024
+            collective_id=0, has_side_effects=True, vmem_limit_bytes=64 * 1024 * 1024
         ),
         cost_estimate=pl.CostEstimate(
             flops=2 * 1024 * 2048 * 384, bytes_accessed=1 << 20, transcendentals=1024 * 2048

time: 37.9 us -> 33.2 us (0.88); the launches traced: 37.4 us -> 33 us
  local copies, waits for them, and re-layouts: 3.25 us -> 0 us
  Pallas kernels: 32.9 us -> 30 us
  matrix products: 1.23 us -> 3.01 us
    unnamed x10 -> x0, local copies, waits for them, and re-layouts: 3.25 us -> none
    pallas_call x1, Pallas kernels: 32.9 us -> 30 us  [by_head(): pl.pallas_call(functools.partial(head_kernel, devices), name='attend', ou...]
    dot_general x1, matrix products: 1.23 us -> 3.01 us  [by_head(): jnp.dot(attended, out_weight, preferred_element_type=jnp.float32)]
where the time goes in v3:
time: 33.2 us; the launch traced here: 33 us
  Pallas kernels  30 us (90%)
  matrix products  3.01 us (9%)
    pallas_call x1, Pallas kernels, by_head(): pl.pallas_call(functools.partial(head_kernel, devices), name='attend', ou...  30 us
    dot_general x1, matrix products, by_head(): jnp.dot(attended, out_weight, preferred_element_type=jnp.float32)  3.01 us

profile of v3, /device:TPU:0, one launch (start us, length us, event | category | flops | bytes accessed | tf_op | source)
XLA Modules:
  0.0 33.0 jit_solution(13746520402349259412)
XLA Ops:
  0.0 30.0 %attend.1 = bf16[128,768]{1,0:T(8,128)(2,1)} custom-call(bf16[128,2304]{1,0:T(8,128)(2,1)} %qkv_hbm.1, s32[16,16]{1,0:T(8,128)} %pair_hbm.1, s32[2,16]{1,0:T(2,128)} %dims_hbm.1, s32[1,7]{1,0:T(1,128)} %mask_hbm.1), custom_call_target="tpu_custom_call" | custom-call | flops 1610612736 | bytes 1048576 | tf_op jit(solution)/shard_map/attend/pallas_call | solution.py:520
  30.0 3.0 %convolution_convert_fusion = bf16[128,1536]{1,0:T(8,128)(2,1)} fusion(bf16[128,768]{1,0:T(8,128)(2,1)} %attend.1, bf16[768,1536]{1,0:T(8,128)(2,1)} %param.9), kind=kOutput, calls=%fused_computation | convolution fusion | flops 302186496 | bytes 2949120 | tf_op jit(solution)/shard_map/dot_general | solution.py:558
